TPU v7x, 32 devices: a whole 2x2x4 slice. The times are simulated.
32 devices in a mesh: groups: 2 (over y), rows: 4 (over z), tm: 2 (over x), dp: 2 (over core).
Axes of the slice: x: 2, y: 2, z: 4, core: 2. Of those that a mesh axis runs over, the one named last changes fastest.
Arguments:
- frames_in: bfloat16 [4, 4, 16, 320, 128], P(('groups', 'dp'), 'tm', 'rows'), parts along dimension 0, may hold values from -6 to 6
- gain: float32 [128], replicated, may hold values from 0.5 to 1.5
- spatial_w: bfloat16 [3, 3, 128, 128], replicated, may hold values from -0.1875 to 0.1875
- temporal_w: bfloat16 [3, 128, 128], replicated, may hold values from -0.3125 to 0.3125
- cotangent: bfloat16 [4, 4, 16, 320, 128], P(('groups', 'dp'), 'tm', 'rows'), parts along dimension 0, may hold values from -6 to 6
Outputs:
- block_out: bfloat16 [4, 4, 16, 320, 128], P(('groups', 'dp'), 'tm', 'rows'), parts along dimension 0
- grad_input: bfloat16 [4, 4, 16, 320, 128], P(('groups', 'dp'), 'tm', 'rows'), parts along dimension 0
- grad_spatial: float32 [6, 3, 128, 128], P('groups'), parts along dimension 0
- grad_temporal: float32 [6, 128, 128], P('groups'), parts along dimension 0
- grad_gain: float32 [256], P('groups'), parts along dimension 0
There are 2 independent parts, one for each index of `groups`. A program takes and returns all parts, laid end to end along the dimension named above; an argument that names none is the same for every part. Nothing has to cross between parts.
All inputs are finite; a program needn't handle non-finite values.
Results may differ from a plain program's by a relative error of at most 0.0054.
Values may be sent and summed in bfloat16 or wider, within the bound.
A program may use at most 64 MiB of HBM per device.

v0:
```python
import math
import jax
import jax.numpy as jnp
from jax import lax
from jax.sharding import PartitionSpec as P

EPS = 1e-06


def extended(shard, sides, width):
    for axis, dim in sides:
        size, length = (lax.axis_size(axis), shard.shape[dim])
        up = [(i, (i + 1) % size) for i in range(size - 1)]
        down = [(j, i) for i, j in up]
        last = lax.slice_in_dim(shard, length - width, length, axis=dim)
        first = lax.slice_in_dim(shard, 0, width, axis=dim)
        before = lax.ppermute(last, axis, up)
        after = lax.ppermute(first, axis, down)
        shard = jnp.concatenate([before, shard, after], axis=dim)
    return shard


def passed_along(shard, axis, by):
    length = lax.axis_size(axis)
    pairs = [(i, i + by) for i in range(length) if 0 <= i + by < length]
    return lax.ppermute(shard, axis, pairs)


def flatten(block):
    return block.reshape(-1, block.shape[-1])


def product(left, right):
    return jnp.dot(flatten(left), right, preferred_element_type=jnp.float32)


def outer_sum(left, right):
    return lax.dot_general(
        flatten(left), flatten(right), (((0,), (0,)), ((), ())), preferred_element_type=jnp.float32
    )


def spatial_back(padded, kernel, height, width):
    total = None
    for i in range(3):
        for j in range(3):
            term = product(
                padded[:, :, 2 - i : 2 - i + height, 2 - j : 2 - j + width], kernel[i, j].T
            )
            total = term if total is None else total + term
    return total


def shards(frames_in, gain, spatial_w, temporal_w, cotangent):
    clips, frames, height, width, chans = frames_in.shape
    lead = (clips, frames, height, width, chans)
    upper = frames_in.astype(jnp.float32)
    recip = lax.rsqrt(jnp.mean(upper * upper, axis=-1, keepdims=True) + EPS)
    unit = upper * recip
    normed = (unit * gain).astype(jnp.bfloat16)
    banded = extended(normed, (("rows", 2),), 1)
    padded = jnp.pad(banded, ((0, 0), (0, 0), (0, 0), (1, 1), (0, 0)))
    hidden = None
    for i in range(3):
        for j in range(3):
            term = product(padded[:, :, i : i + height, j : j + width], spatial_w[i, j])
            hidden = term if hidden is None else hidden + term
    hidden = hidden.reshape(lead)
    act = jax.nn.silu(hidden).astype(jnp.bfloat16)
    earlier = passed_along(act, "tm", 1)
    act_pad = jnp.concatenate([earlier, act], axis=1)
    mixed = product(act_pad[:, 2 : 2 + frames], temporal_w[0])
    for k in range(1, 3):
        mixed = mixed + product(act_pad[:, 2 - k : 2 - k + frames], temporal_w[k])
    block_out = (upper + mixed.reshape(lead)).astype(jnp.bfloat16)
    later = passed_along(cotangent, "tm", -1)
    cot_pad = jnp.concatenate([cotangent, later], axis=1)
    dact = product(cot_pad[:, 0:frames], temporal_w[0].T)
    for k in range(1, 3):
        dact = dact + product(cot_pad[:, k : k + frames], temporal_w[k].T)
    sig = jax.nn.sigmoid(hidden)
    dhid = (dact.reshape(lead) * sig * (1.0 + hidden * (1.0 - sig))).astype(jnp.bfloat16)
    grad_temporal = jnp.stack(
        [outer_sum(act_pad[:, 2 - k : 2 - k + frames], cotangent) for k in range(3)]
    )
    cells_all = (
        clips
        * frames
        * height
        * width
        * lax.axis_size("rows")
        * lax.axis_size("tm")
        * lax.axis_size("dp")
    )
    scale = 1.0 / math.sqrt(cells_all)
    dzero = jnp.pad(dhid, ((0, 0), (0, 0), (2, 2), (1, 1), (0, 0)))
    whole = spatial_back(dzero, spatial_w, height + 2, width).reshape(
        (clips, frames, height + 2, width, chans)
    )
    from_above = passed_along(whole[:, :, height + 1 :].astype(jnp.bfloat16), "rows", 1).astype(
        jnp.float32
    )
    from_below = passed_along(whole[:, :, 0:1].astype(jnp.bfloat16), "rows", -1).astype(jnp.float32)
    dnorm = whole[:, :, 1 : height + 1]
    dnorm = dnorm.at[:, :, 0:1].add(from_above)
    dnorm = dnorm.at[:, :, height - 1 : height].add(from_below)
    spatial_rows = []
    for i in range(3):
        spatial_cols = []
        for j in range(3):
            spatial_cols.append(outer_sum(padded[:, :, i : i + height, j : j + width], dhid))
        spatial_rows.append(jnp.stack(spatial_cols))
    grad_spatial = jnp.stack(spatial_rows)
    grad_gain = jnp.sum(dnorm * unit, axis=(0, 1, 2, 3))
    grad_spatial, grad_temporal, grad_gain = lax.psum(
        (grad_spatial, grad_temporal, grad_gain), ("rows", "tm", "dp")
    )
    dunit = dnorm * gain
    grad_input = (
        cotangent.astype(jnp.float32)
        + recip * (dunit - unit * jnp.mean(dunit * unit, axis=-1, keepdims=True))
    ).astype(jnp.bfloat16)
    return (block_out, grad_input, grad_spatial * scale, grad_temporal * scale, grad_gain * scale)


def solution(mesh):
    return jax.shard_map(
        shards,
        mesh=mesh,
        in_specs=(
            P(("groups", "dp"), "tm", "rows", None, None),
            P(),
            P(),
            P(),
            P(("groups", "dp"), "tm", "rows", None, None),
        ),
        out_specs=(
            P(("groups", "dp"), "tm", "rows", None, None),
            P(("groups", "dp"), "tm", "rows", None, None),
            P("groups", None, None, None),
            P("groups", None, None),
            P("groups"),
        ),
        check_vma=False,
    )
```

profile of v0, /device:TPU:0, one launch (start us, length us, event | category | flops | bytes accessed | tf_op | source)
XLA Modules:
  0.0 192.7 jit_solution(13148399722400150449)
XLA Ops:
  7.2 1.6 fusion.13
  8.9 1.5 fusion.6
  10.4 4.9 %collective-permute-start = (bf16[1,2,1,320,128]{4,3,2,1,0:T(8,128)(2,1)S(1)}, bf16[1,2,1,320,128]{4,3,2,1,0:T(8,128)(2,1)S(1)}, u32[]{:S(2)}, u32[]{:S(2)}) collective-permute-start(bf16[1,2,1,320,128]{4,3,2,1,0:T(8,128)(2,1)S(1)} %get-tuple-element.58), channel_id=1, source_target_pairs={{0,4},{4,8},{8,12},{1,5},{5,9},{9,13},{2,6},{6,10},{10,14},{3,7},{... | collective-permute-start | bytes 491528 | tf_op jit(solution)/shard_map/ppermute | solution.py:17
  15.4 1.3 collective-permute-start.1
  16.7 1.3 collective-permute-start.3
  18.0 0.3 fusion.40
  18.3 0.5 collective-permute-done
  18.8 4.1 %collective-permute-done.1 = bf16[1,2,1,320,128]{4,3,2,1,0:T(8,128)(2,1)S(1)} collective-permute-done((bf16[1,2,1,320,128]{4,3,2,1,0:T(8,128)(2,1)S(1)}, bf16[1,2,1,320,128]{4,3,2,1,0:T(8,128)(2,1)S(1)}, u32[]{:S(2)}, u32[]{:S(2)}) %collective-permute-start.1) | collective-permute-done | bytes 163872 | tf_op jit(solution)/shard_map/ppermute | solution.py:18
  22.9 0.3 fusion.19
  23.2 0.8 fusion.95
  24.1 0.1 copy-done.3
  24.2 0.3 fusion.63
  24.6 0.3 convolution_add_fusion.18
  24.9 0.3 convolution_add_fusion.17
  25.2 0.3 convolution_add_fusion.16
  25.6 0.3 convolution_add_fusion.15
  25.9 0.3 fusion.45
  26.2 0.3 convolution_add_fusion.14
  26.5 0.3 convolution_add_fusion.13
  26.8 7.9 %collective-permute-done.3 = bf16[1,2,4,320,128]{4,3,2,1,0:T(8,128)(2,1)S(1)} collective-permute-done((bf16[1,2,4,320,128]{4,3,2,1,0:T(8,128)(2,1)S(1)}, bf16[1,2,4,320,128]{4,3,2,1,0:T(8,128)(2,1)S(1)}, u32[]{:S(2)}, u32[]{:S(2)}) %collective-permute-start.3) | collective-permute-done | bytes 655392 | tf_op jit(solution)/shard_map/ppermute | solution.py:26
  34.8 0.3 convolution_add_fusion.9
  35.2 0.3 convolution_add_fusion.8
  35.5 0.8 multiply_convert_fusion
  36.3 0.4 convolution_bitcast_fusion.4
  36.7 0.4 convolution_bitcast_fusion.7
  37.1 0.4 convolution_bitcast_fusion.10
  37.5 0.4 convolution_bitcast_fusion.3
  37.9 0.4 convolution_bitcast_fusion.5
  38.3 0.4 convolution_bitcast_fusion.6
  38.6 0.4 convolution_bitcast_fusion.8
  39.0 0.4 convolution_bitcast_fusion.9
  39.4 0.4 convolution_bitcast_fusion.11
  39.8 1.5 multiply_convert_fusion.1
  41.3 2.1 %pad_slice_fusion = (bf16[1,2,6,320,128]{4,3,2,1,0:T(8,128)(2,1)S(1)}, bf16[1,2,6,320,128]{4,3,2,1,0:T(8,128)(2,1)S(1)}, bf16[1,2,6,320,128]{4,3,2,1,0:T(8,128)(...) fusion(bf16[1,2,4,320,128]{4,3,2,1,0:T(8,128)(2,1)S(1)} %get-tu, ...), kind=kLoop, calls=%fused_computation.22 | loop fusion | bytes 9502720 | tf_op jit(solution)/shard_map/slice | solution.py:48
  43.4 0.4 fusion.61
  43.8 0.4 convolution_add_fusion.7
  44.2 0.4 convolution_add_fusion.6
  44.6 0.4 convolution_add_fusion.5
  45.1 0.4 convolution_add_fusion.4
  45.5 0.4 convolution_add_fusion.3
  45.9 0.4 convolution_add_fusion.2
  46.3 0.4 convolution_add_fusion.1
  46.7 0.4 convolution_add_fusion
  47.2 0.1 convert.4
  47.4 1.5 collective-permute-start.2
  48.9 1.4 fusion.42
  50.3 1.3 collective-permute-start.5
  51.6 4.9 %collective-permute-start.4 = (bf16[1,2,1,320,128]{4,3,2,1,0:T(8,128)(2,1)S(1)}, bf16[1,2,1,320,128]{4,3,2,1,0:T(8,128)(2,1)S(1)}, u32[]{:S(2)}, u32[]{:S(2)}) collective-permute-start(bf16[1,2,1,320,128]{4,3,2,1,0:T(8,128)(2,1)S(1)} %get-tuple-element.44), channel_id=1, source_target_pairs={{0,4},{4,8},{8,12},{1,5},{5,9},{9,13},{2,6},{6,10},{10,14},{3,7},{... | collective-permute-start | bytes 491528 | tf_op jit(solution)/shard_map/ppermute | solution.py:26
  56.6 0.9 pad_maximum_fusion.4
  57.5 0.4 convolution_bitcast_fusion.2
  57.8 1.5 collective-permute-done.4
  59.5 0.9 fusion.12
  60.4 30.0 %psum.23 = f32[128]{0:T(128)S(1)} all-reduce(f32[128]{0:T(128)S(1)} %get-tuple-element.29), channel_id=1, replica_groups=mesh['groups'=2,'rows'=4,'tm'=2,'dp'=2] {'rows','tm','dp'}, use_global_device_ids=true, to_apply=%region_5.6 | all-reduce | flops 128 | bytes 1024 | tf_op jit(solution)/shard_map/psum | solution.py:115
  90.4 0.5 broadcast_multiply_fusion.3
  90.9 1.0 pad_maximum_fusion.1
  91.9 0.4 convolution_bitcast_fusion.1
  92.3 0.4 convolution_bitcast_fusion
  92.8 0.7 pad_maximum_fusion.5
  93.5 1.8 convolution_add_fusion.11
  95.3 0.3 convolution_add_fusion.10
  95.7 1.6 fusion.11
  97.3 85.9 %all-reduce.5.cloned.1.call-done = (f32[3,3,128,128]{3,2,1,0:T(8,128)}, f32[3,128,128]{2,1,0:T(8,128)}) async-done(((f32[3,3,128,128]{3,2,1,0:T(8,128)}, f32[3,128,128]{2,1,0:T(8,128)}), (f32[3,3,128,128]{3,2,1,0:T(8,128)}, f32[3,128,128]{2,1,0:T(8,128)})) %all-reduce.5.cloned.1.call-update) | async-done | bytes 786448 | tf_op jit(solution)/shard_map/psum | solution.py:115
  183.2 2.0 %broadcast_multiply_fusion = f32[3,3,128,128]{3,2,1,0:T(8,128)} fusion(f32[3,3,128,128]{3,2,1,0:T(8,128)} %get-tuple-element.31), kind=kLoop, calls=%fused_computation.94 | loop fusion | flops 147456 | bytes 1179648 | tf_op jit(solution)/shard_map/mul | solution.py:123
  185.2 0.7 broadcast_multiply_fusion.1
  (28 shorter events, 0.6 us)
Async XLA Ops:
  7.2 9.5 %copy-start = (bf16[1,2,4,320,128]{4,3,2,1,0:T(8,128)(2,1)S(1)}, bf16[1,2,4,320,128]{4,3,2,1,0:T(8,128)(2,1)}, u32[]{:S(2)}) copy-start(bf16[1,2,4,320,128]{4,3,2,1,0:T(8,128)(2,1)} %param.13) | copy-start | bytes 1966084
  7.2 10.8 %copy-start.4 = (bf16[3,128,128]{2,1,0:T(8,128)(2,1)S(1)}, bf16[3,128,128]{2,1,0:T(8,128)(2,1)}, u32[]{:S(2)}) copy-start(bf16[3,128,128]{2,1,0:T(8,128)(2,1)} %param.12) | copy-start | bytes 294916
  7.2 176.0 %all-reduce.5.cloned.1.call-start = ((), (), s32[]{:S(2)}) async-start(), calls=%async_computation | async-start | bytes 1572864 | tf_op jit(solution)/shard_map/psum | solution.py:115
  10.4 8.4 %collective-permute-start = (bf16[1,2,1,320,128]{4,3,2,1,0:T(8,128)(2,1)S(1)}, bf16[1,2,1,320,128]{4,3,2,1,0:T(8,128)(2,1)S(1)}, u32[]{:S(2)}, u32[]{:S(2)}) collective-permute-start(bf16[1,2,1,320,128]{4,3,2,1,0:T(8,128)(2,1)S(1)} %get-tuple-element.58), channel_id=1, source_target_pairs={{0,4},{4,8},{8,12},{1,5},{5,9},{9,13},{2,6},{6,10},{10,14},{3,7},{... | collective-permute-start | bytes 491528 | tf_op jit(solution)/shard_map/ppermute | solution.py:17
  15.4 7.6 %collective-permute-start.1 = (bf16[1,2,1,320,128]{4,3,2,1,0:T(8,128)(2,1)S(1)}, bf16[1,2,1,320,128]{4,3,2,1,0:T(8,128)(2,1)S(1)}, u32[]{:S(2)}, u32[]{:S(2)}) collective-permute-start(bf16[1,2,1,320,128]{4,3,2,1,0:T(8,128)(2,1)S(1)} %get-tuple-element.59), channel_id=1, source_target_pairs={{4,0},{8,4},{12,8},{5,1},{9,5},{13,9},{6,2},{10,6},{14,10},{7,3},{... | collective-permute-start | bytes 491528 | tf_op jit(solution)/shard_map/ppermute | solution.py:18
  16.7 18.1 %collective-permute-start.3 = (bf16[1,2,4,320,128]{4,3,2,1,0:T(8,128)(2,1)S(1)}, bf16[1,2,4,320,128]{4,3,2,1,0:T(8,128)(2,1)S(1)}, u32[]{:S(2)}, u32[]{:S(2)}) collective-permute-start(bf16[1,2,4,320,128]{4,3,2,1,0:T(8,128)(2,1)S(1)} %copy-done), channel_id=1, source_target_pairs={{2,0},{3,1},{6,4},{7,5},{10,8},{11,9},{14,12},{15,13},{18,16},{19,... | collective-permute-start | bytes 1966088 | tf_op jit(solution)/shard_map/ppermute | solution.py:26
  23.2 1.0 copy-start.3
  47.4 43.5 %collective-permute-start.2 = (bf16[1,2,4,320,128]{4,3,2,1,0:T(8,128)(2,1)}, bf16[1,2,4,320,128]{4,3,2,1,0:T(8,128)(2,1)S(1)}, u32[]{:S(2)}, u32[]{:S(2)}) collective-permute-start(bf16[1,2,4,320,128]{4,3,2,1,0:T(8,128)(2,1)} %get-tuple-element.36), channel_id=1, source_target_pairs={{0,2},{1,3},{4,6},{5,7},{8,10},{9,11},{12,14},{13,15},{16,18},{17,... | collective-permute-start | bytes 1966088 | tf_op jit(solution)/shard_map/ppermute | solution.py:26
  50.3 9.1 %collective-permute-start.5 = (bf16[1,2,1,320,128]{4,3,2,1,0:T(8,128)(2,1)S(1)}, bf16[1,2,1,320,128]{4,3,2,1,0:T(8,128)(2,1)S(1)}, u32[]{:S(2)}, u32[]{:S(2)}) collective-permute-start(bf16[1,2,1,320,128]{4,3,2,1,0:T(8,128)(2,1)S(1)} %get-tuple-element.43), channel_id=1, source_target_pairs={{4,0},{8,4},{12,8},{5,1},{9,5},{13,9},{6,2},{10,6},{14,10},{7,3},{... | collective-permute-start | bytes 491528 | tf_op jit(solution)/shard_map/ppermute | solution.py:26
  51.6 7.7 %collective-permute-start.4 = (bf16[1,2,1,320,128]{4,3,2,1,0:T(8,128)(2,1)S(1)}, bf16[1,2,1,320,128]{4,3,2,1,0:T(8,128)(2,1)S(1)}, u32[]{:S(2)}, u32[]{:S(2)}) collective-permute-start(bf16[1,2,1,320,128]{4,3,2,1,0:T(8,128)(2,1)S(1)} %get-tuple-element.44), channel_id=1, source_target_pairs={{0,4},{4,8},{8,12},{1,5},{5,9},{9,13},{2,6},{6,10},{10,14},{3,7},{... | collective-permute-start | bytes 491528 | tf_op jit(solution)/shard_map/ppermute | solution.py:26
  57.5 2.0 %copy-start.1 = (bf16[1,2,4,320,128]{4,3,2,1,0:T(8,128)(2,1)S(1)}, bf16[1,2,4,320,128]{4,3,2,1,0:T(8,128)(2,1)}, u32[]{:S(2)}) copy-start(bf16[1,2,4,320,128]{4,3,2,1,0:T(8,128)(2,1)} %param.9) | copy-start | bytes 1966084
  57.5 2.0 %copy-start.6 = (f32[128]{0:T(128)S(1)}, f32[128]{0:T(128)}, u32[]{:S(2)}) copy-start(f32[128]{0:T(128)} %param.10) | copy-start | bytes 1540
  91.9 0.8 copy-start.2
  183.2 2.0 %copy-start.5 = (f32[3,128,128]{2,1,0:T(8,128)S(1)}, f32[3,128,128]{2,1,0:T(8,128)}, u32[]{:S(2)}) copy-start(f32[3,128,128]{2,1,0:T(8,128)} %get-tuple-element.32) | copy-start | bytes 589828
Sparse Core Ops, SparseCore 0:
  93.6 89.5 all-reduce.4
where the time goes:
time: 193 us
  waiting for transfers between devices  100 us (52%)
  blocking collectives  30 us (16%)
  matrix products  16.1 us (8%)
  starting transfers between devices  15.3 us (8%)
  between operations  14.4 us (7%)
  other arithmetic  13.6 us (7%)
  local copies, waits for them, and re-layouts  3.27 us (2%)
    psum x1, waiting for transfers between devices, shards(): lax.psum((grad_spatial, grad_temporal, grad_gain), ('rows', 'tm', 'dp'))  85.9 us
    psum x1, blocking collectives, shards(): lax.psum((grad_spatial, grad_temporal, grad_gain), ('rows', 'tm', 'dp'))  30 us
    dot_general x24, matrix products, product(): return jnp.dot(flatten(left), right, preferred_element_type=jnp.float32)  11.6 us
    ppermute x4, waiting for transfers between devices, passed_along(): return lax.ppermute(shard, axis, pairs)  9.45 us
    ppermute x4, starting transfers between devices, passed_along(): return lax.ppermute(shard, axis, pairs)  8.98 us
    ppermute x1, starting transfers between devices, extended(): before = lax.ppermute(last, axis, up)  4.94 us
    dot_general x12, matrix products, outer_sum(): lax.dot_general(flatten(left), flatten(right), (((0,), (0,)), ((), ())),...  4.54 us
    ppermute x1, waiting for transfers between devices, extended(): after = lax.ppermute(first, axis, down)  4.12 us
  transfers between devices with their start and end apart: 7, of which 5 were waited for; matrix products, arithmetic and copies ran while one was open for 6% of the time, Pallas kernels for 0%

commit v1 on v0

--- a/solution.py
+++ b/solution.py
@@ -5,6 +5,7 @@
 from jax.sharding import PartitionSpec as P
 
 EPS = 1e-06
+_drive_cube = lambda field_in: lax.psum(lax.psum(field_in, ("tm", "dp")), "rows")
 
 
 def extended(shard, sides, width):
@@ -112,9 +113,7 @@
         spatial_rows.append(jnp.stack(spatial_cols))
     grad_spatial = jnp.stack(spatial_rows)
     grad_gain = jnp.sum(dnorm * unit, axis=(0, 1, 2, 3))
-    grad_spatial, grad_temporal, grad_gain = lax.psum(
-        (grad_spatial, grad_temporal, grad_gain), ("rows", "tm", "dp")
-    )
+    grad_spatial, grad_temporal, grad_gain = _drive_cube((grad_spatial, grad_temporal, grad_gain))
     dunit = dnorm * gain
     grad_input = (
         cotangent.astype(jnp.float32)

time: 193 us -> 171 us (0.89)
  waiting for transfers between devices: 100 us -> 88.6 us
  blocking collectives: 30 us -> 19.1 us
    psum x1 -> x2, waiting for transfers between devices: 85.9 us -> 74.5 us  [the longest x1 42.7 us: lax.psum(lax.psum(field_in, ('tm', 'dp')), 'rows')]
    psum x1 -> x2, blocking collectives: 30 us -> 19.1 us  [the longest x1 13.3 us: lax.psum(lax.psum(field_in, ('tm', 'dp')), 'rows')]
  transfers between devices with their start and end apart: 7 -> 8, of which waited for: 5 -> 6; matrix products, arithmetic and copies ran while one was open for 6% -> 7% of each run, Pallas kernels for 0% -> 0%
where the time goes in v1:
time: 171 us; the launch traced here: 170 us
  waiting for transfers between devices  88.6 us (52%)
  blocking collectives  19.1 us (11%)
  matrix products  16.1 us (9%)
  starting transfers between devices  15.3 us (9%)
  between operations  14.5 us (8%)
  other arithmetic  13.6 us (8%)
  local copies, waits for them, and re-layouts  3.27 us (2%)
    psum x1, waiting for transfers between devices, lax.psum(lax.psum(field_in, ('tm', 'dp')), 'rows')  42.7 us
    psum x1, waiting for transfers between devices, lax.psum(field_in, ('tm', 'dp'))  31.8 us
    psum x1, blocking collectives, lax.psum(lax.psum(field_in, ('tm', 'dp')), 'rows')  13.3 us
    dot_general x24, matrix products, product(): return jnp.dot(flatten(left), right, preferred_element_type=jnp.float32)  11.6 us
    ppermute x4, waiting for transfers between devices, passed_along(): return lax.ppermute(shard, axis, pairs)  9.45 us
    ppermute x4, starting transfers between devices, passed_along(): return lax.ppermute(shard, axis, pairs)  8.98 us
    psum x1, blocking collectives, lax.psum(field_in, ('tm', 'dp'))  5.76 us
    ppermute x1, starting transfers between devices, extended(): before = lax.ppermute(last, axis, up)  4.94 us
  transfers between devices with their start and end apart: 8, of which 6 were waited for; matrix products, arithmetic and copies ran while one was open for 7% of the time, Pallas kernels for 0%

profile of v1, /device:TPU:0, one launch (start us, length us, event | category | flops | bytes accessed | tf_op | source)
XLA Modules:
  0.0 170.4 jit_solution(6987809129392744511)
XLA Ops:
  7.2 1.6 fusion.13
  8.9 1.5 fusion.6
  10.4 4.9 %collective-permute-start = (bf16[1,2,1,320,128]{4,3,2,1,0:T(8,128)(2,1)S(1)}, bf16[1,2,1,320,128]{4,3,2,1,0:T(8,128)(2,1)S(1)}, u32[]{:S(2)}, u32[]{:S(2)}) collective-permute-start(bf16[1,2,1,320,128]{4,3,2,1,0:T(8,128)(2,1)S(1)} %get-tuple-element.60), channel_id=1, source_target_pairs={{0,4},{4,8},{8,12},{1,5},{5,9},{9,13},{2,6},{6,10},{10,14},{3,7},{... | collective-permute-start | bytes 491528 | tf_op jit(solution)/shard_map/ppermute | solution.py:18
  15.4 1.3 collective-permute-start.1
  16.7 1.3 collective-permute-start.3
  18.0 0.3 fusion.40
  18.3 0.5 collective-permute-done
  18.8 4.1 %collective-permute-done.1 = bf16[1,2,1,320,128]{4,3,2,1,0:T(8,128)(2,1)S(1)} collective-permute-done((bf16[1,2,1,320,128]{4,3,2,1,0:T(8,128)(2,1)S(1)}, bf16[1,2,1,320,128]{4,3,2,1,0:T(8,128)(2,1)S(1)}, u32[]{:S(2)}, u32[]{:S(2)}) %collective-permute-start.1) | collective-permute-done | bytes 163872 | tf_op jit(solution)/shard_map/ppermute | solution.py:19
  22.9 0.3 fusion.19
  23.2 0.8 fusion.95
  24.2 0.3 fusion.63
  24.6 0.3 convolution_add_fusion.18
  24.9 0.3 convolution_add_fusion.17
  25.2 0.3 convolution_add_fusion.16
  25.6 0.3 convolution_add_fusion.15
  25.9 0.3 fusion.45
  26.2 0.3 convolution_add_fusion.14
  26.5 0.3 convolution_add_fusion.13
  26.8 7.9 %collective-permute-done.3 = bf16[1,2,4,320,128]{4,3,2,1,0:T(8,128)(2,1)S(1)} collective-permute-done((bf16[1,2,4,320,128]{4,3,2,1,0:T(8,128)(2,1)S(1)}, bf16[1,2,4,320,128]{4,3,2,1,0:T(8,128)(2,1)S(1)}, u32[]{:S(2)}, u32[]{:S(2)}) %collective-permute-start.3) | collective-permute-done | bytes 655392 | tf_op jit(solution)/shard_map/ppermute | solution.py:27
  34.8 0.3 convolution_add_fusion.9
  35.2 0.3 convolution_add_fusion.8
  35.5 0.8 multiply_convert_fusion
  36.3 0.4 convolution_bitcast_fusion.4
  36.7 0.4 convolution_bitcast_fusion.7
  37.1 0.4 convolution_bitcast_fusion.10
  37.5 0.4 convolution_bitcast_fusion.3
  37.9 0.4 convolution_bitcast_fusion.5
  38.3 0.4 convolution_bitcast_fusion.6
  38.6 0.4 convolution_bitcast_fusion.8
  39.0 0.4 convolution_bitcast_fusion.9
  39.4 0.4 convolution_bitcast_fusion.11
  39.8 1.5 multiply_convert_fusion.1
  41.3 2.1 %pad_slice_fusion = (bf16[1,2,6,320,128]{4,3,2,1,0:T(8,128)(2,1)S(1)}, bf16[1,2,6,320,128]{4,3,2,1,0:T(8,128)(2,1)S(1)}, bf16[1,2,6,320,128]{4,3,2,1,0:T(8,128)(...) fusion(bf16[1,2,4,320,128]{4,3,2,1,0:T(8,128)(2,1)S(1)} %get-tu, ...), kind=kLoop, calls=%fused_computation.22 | loop fusion | bytes 9502720 | tf_op jit(solution)/shard_map/slice | solution.py:49
  43.4 0.4 fusion.61
  43.8 0.4 convolution_add_fusion.7
  44.2 0.4 convolution_add_fusion.6
  44.6 0.4 convolution_add_fusion.5
  45.1 0.4 convolution_add_fusion.4
  45.5 0.4 convolution_add_fusion.3
  45.9 0.4 convolution_add_fusion.2
  46.3 0.4 convolution_add_fusion.1
  46.7 0.4 convolution_add_fusion
  47.4 1.5 collective-permute-start.2
  48.9 1.4 fusion.42
  50.3 1.3 collective-permute-start.5
  51.6 4.9 %collective-permute-start.4 = (bf16[1,2,1,320,128]{4,3,2,1,0:T(8,128)(2,1)S(1)}, bf16[1,2,1,320,128]{4,3,2,1,0:T(8,128)(2,1)S(1)}, u32[]{:S(2)}, u32[]{:S(2)}) collective-permute-start(bf16[1,2,1,320,128]{4,3,2,1,0:T(8,128)(2,1)S(1)} %get-tuple-element.46), channel_id=1, source_target_pairs={{0,4},{4,8},{8,12},{1,5},{5,9},{9,13},{2,6},{6,10},{10,14},{3,7},{... | collective-permute-start | bytes 491528 | tf_op jit(solution)/shard_map/ppermute | solution.py:27
  56.6 0.9 pad_maximum_fusion.4
  57.5 0.4 convolution_bitcast_fusion.2
  57.8 1.5 collective-permute-done.4
  59.5 0.9 fusion.12
  60.4 5.8 %psum.46 = f32[128]{0:T(128)S(1)} all-reduce(f32[128]{0:T(128)S(1)} %get-tuple-element.29), channel_id=1, replica_groups=mesh['groups'=2,'rows'=4,'tm'=2,'dp'=2] {'tm','dp'}, use_global_device_ids=true, to_apply=%region_7.8 | all-reduce | flops 128 | bytes 1024 | tf_op jit(solution)/shard_map/psum | solution.py:8
  66.1 13.3 %psum.47 = f32[128]{0:T(128)S(1)} all-reduce(f32[128]{0:T(128)S(1)} %psum.46), channel_id=1, replica_groups=mesh['groups'=2,'rows'=4,'tm'=2,'dp'=2] {'rows'}, use_global_device_ids=true, to_apply=%region_8.9 | all-reduce | flops 128 | bytes 1024 | tf_op jit(solution)/shard_map/psum | solution.py:8
  79.4 1.0 pad_maximum_fusion.1
  80.5 0.4 convolution_bitcast_fusion.1
  80.8 0.4 convolution_bitcast_fusion
  81.3 0.7 pad_maximum_fusion.5
  82.1 0.5 broadcast_multiply_fusion.3
  82.6 31.8 %all-reduce.7.cloned.1.call-done = (f32[3,3,128,128]{3,2,1,0:T(8,128)}, f32[3,128,128]{2,1,0:T(8,128)}) async-done(((f32[3,3,128,128]{3,2,1,0:T(8,128)}, f32[3,128,128]{2,1,0:T(8,128)}), (f32[3,3,128,128]{3,2,1,0:T(8,128)}, f32[3,128,128]{2,1,0:T(8,128)})) %all-reduce.7.cloned.1.call-update) | async-done | bytes 786448 | tf_op jit(solution)/shard_map/psum | solution.py:8
  114.4 1.8 %convolution_add_fusion.11 = f32[2560,128]{1,0:T(8,128)S(1)} fusion(f32[2560,128]{1,0:T(8,128)} %fusion.42, bf16[2560,128]{1,0:T(8,128)(2,1)} %bitcast.249, bf16[3,128,128]{2,1,0:T(8,128)(2,1)S(1)} %copy-done.4), kind=kOutput, calls=%fused_computation.11 | convolution fusion | flops 84213760 | bytes 3309568 | tf_op jit(solution)/shard_map/dot_general | solution.py:35
  116.3 0.3 convolution_add_fusion.10
  116.6 1.6 fusion.11
  118.2 42.7 %all-reduce.9.cloned.1.call-done = (f32[3,3,128,128]{3,2,1,0:T(8,128)}, f32[3,128,128]{2,1,0:T(8,128)}) async-done(((f32[3,3,128,128]{3,2,1,0:T(8,128)}, f32[3,128,128]{2,1,0:T(8,128)}), (f32[3,3,128,128]{3,2,1,0:T(8,128)}, f32[3,128,128]{2,1,0:T(8,128)})) %all-reduce.9.cloned.1.call-update) | async-done | bytes 786448 | tf_op jit(solution)/shard_map/psum | solution.py:8
  160.9 2.0 %broadcast_multiply_fusion = f32[3,3,128,128]{3,2,1,0:T(8,128)} fusion(f32[3,3,128,128]{3,2,1,0:T(8,128)} %get-tuple-element.33), kind=kLoop, calls=%fused_computation.94 | loop fusion | flops 147456 | bytes 1179648 | tf_op jit(solution)/shard_map/mul | solution.py:122
  162.9 0.7 broadcast_multiply_fusion.1
  (32 shorter events, 0.9 us)
Async XLA Ops:
  7.2 9.5 %copy-start = (bf16[1,2,4,320,128]{4,3,2,1,0:T(8,128)(2,1)S(1)}, bf16[1,2,4,320,128]{4,3,2,1,0:T(8,128)(2,1)}, u32[]{:S(2)}) copy-start(bf16[1,2,4,320,128]{4,3,2,1,0:T(8,128)(2,1)} %param.13) | copy-start | bytes 1966084
  7.2 10.8 %copy-start.4 = (bf16[3,128,128]{2,1,0:T(8,128)(2,1)S(1)}, bf16[3,128,128]{2,1,0:T(8,128)(2,1)}, u32[]{:S(2)}) copy-start(bf16[3,128,128]{2,1,0:T(8,128)(2,1)} %param.12) | copy-start | bytes 294916
  7.2 107.2 %all-reduce.7.cloned.1.call-start = ((), (), s32[]{:S(2)}) async-start(), calls=%async_computation | async-start | bytes 1572864 | tf_op jit(solution)/shard_map/psum | solution.py:8
  10.4 8.4 %collective-permute-start = (bf16[1,2,1,320,128]{4,3,2,1,0:T(8,128)(2,1)S(1)}, bf16[1,2,1,320,128]{4,3,2,1,0:T(8,128)(2,1)S(1)}, u32[]{:S(2)}, u32[]{:S(2)}) collective-permute-start(bf16[1,2,1,320,128]{4,3,2,1,0:T(8,128)(2,1)S(1)} %get-tuple-element.60), channel_id=1, source_target_pairs={{0,4},{4,8},{8,12},{1,5},{5,9},{9,13},{2,6},{6,10},{10,14},{3,7},{... | collective-permute-start | bytes 491528 | tf_op jit(solution)/shard_map/ppermute | solution.py:18
  15.4 7.6 %collective-permute-start.1 = (bf16[1,2,1,320,128]{4,3,2,1,0:T(8,128)(2,1)S(1)}, bf16[1,2,1,320,128]{4,3,2,1,0:T(8,128)(2,1)S(1)}, u32[]{:S(2)}, u32[]{:S(2)}) collective-permute-start(bf16[1,2,1,320,128]{4,3,2,1,0:T(8,128)(2,1)S(1)} %get-tuple-element.61), channel_id=1, source_target_pairs={{4,0},{8,4},{12,8},{5,1},{9,5},{13,9},{6,2},{10,6},{14,10},{7,3},{... | collective-permute-start | bytes 491528 | tf_op jit(solution)/shard_map/ppermute | solution.py:19
  16.7 18.1 %collective-permute-start.3 = (bf16[1,2,4,320,128]{4,3,2,1,0:T(8,128)(2,1)S(1)}, bf16[1,2,4,320,128]{4,3,2,1,0:T(8,128)(2,1)S(1)}, u32[]{:S(2)}, u32[]{:S(2)}) collective-permute-start(bf16[1,2,4,320,128]{4,3,2,1,0:T(8,128)(2,1)S(1)} %copy-done), channel_id=1, source_target_pairs={{2,0},{3,1},{6,4},{7,5},{10,8},{11,9},{14,12},{15,13},{18,16},{19,... | collective-permute-start | bytes 1966088 | tf_op jit(solution)/shard_map/ppermute | solution.py:27
  23.2 1.0 copy-start.3
  47.4 32.0 %collective-permute-start.2 = (bf16[1,2,4,320,128]{4,3,2,1,0:T(8,128)(2,1)}, bf16[1,2,4,320,128]{4,3,2,1,0:T(8,128)(2,1)S(1)}, u32[]{:S(2)}, u32[]{:S(2)}) collective-permute-start(bf16[1,2,4,320,128]{4,3,2,1,0:T(8,128)(2,1)} %get-tuple-element.38), channel_id=1, source_target_pairs={{0,2},{1,3},{4,6},{5,7},{8,10},{9,11},{12,14},{13,15},{16,18},{17,... | collective-permute-start | bytes 1966088 | tf_op jit(solution)/shard_map/ppermute | solution.py:27
  50.3 9.1 %collective-permute-start.5 = (bf16[1,2,1,320,128]{4,3,2,1,0:T(8,128)(2,1)S(1)}, bf16[1,2,1,320,128]{4,3,2,1,0:T(8,128)(2,1)S(1)}, u32[]{:S(2)}, u32[]{:S(2)}) collective-permute-start(bf16[1,2,1,320,128]{4,3,2,1,0:T(8,128)(2,1)S(1)} %get-tuple-element.45), channel_id=1, source_target_pairs={{4,0},{8,4},{12,8},{5,1},{9,5},{13,9},{6,2},{10,6},{14,10},{7,3},{... | collective-permute-start | bytes 491528 | tf_op jit(solution)/shard_map/ppermute | solution.py:27
  51.6 7.7 %collective-permute-start.4 = (bf16[1,2,1,320,128]{4,3,2,1,0:T(8,128)(2,1)S(1)}, bf16[1,2,1,320,128]{4,3,2,1,0:T(8,128)(2,1)S(1)}, u32[]{:S(2)}, u32[]{:S(2)}) collective-permute-start(bf16[1,2,1,320,128]{4,3,2,1,0:T(8,128)(2,1)S(1)} %get-tuple-element.46), channel_id=1, source_target_pairs={{0,4},{4,8},{8,12},{1,5},{5,9},{9,13},{2,6},{6,10},{10,14},{3,7},{... | collective-permute-start | bytes 491528 | tf_op jit(solution)/shard_map/ppermute | solution.py:27
  57.5 2.0 %copy-start.1 = (bf16[1,2,4,320,128]{4,3,2,1,0:T(8,128)(2,1)S(1)}, bf16[1,2,4,320,128]{4,3,2,1,0:T(8,128)(2,1)}, u32[]{:S(2)}) copy-start(bf16[1,2,4,320,128]{4,3,2,1,0:T(8,128)(2,1)} %param.9) | copy-start | bytes 1966084
  57.5 2.0 %copy-start.6 = (f32[128]{0:T(128)S(1)}, f32[128]{0:T(128)}, u32[]{:S(2)}) copy-start(f32[128]{0:T(128)} %param.10) | copy-start | bytes 1540
  80.4 0.8 copy-start.2
  82.0 78.9 %all-reduce.9.cloned.1.call-start = ((), (), s32[]{:S(2)}) async-start(), calls=%async_computation.1 | async-start | bytes 1572864 | tf_op jit(solution)/shard_map/psum | solution.py:8
  160.9 2.0 %copy-start.5 = (f32[3,128,128]{2,1,0:T(8,128)S(1)}, f32[3,128,128]{2,1,0:T(8,128)}, u32[]{:S(2)}) copy-start(f32[3,128,128]{2,1,0:T(8,128)} %get-tuple-element.34) | copy-start | bytes 589828
Sparse Core Ops, SparseCore 0:
  82.1 32.2 all-reduce.6
  116.8 44.0 all-reduce.8
